TPU v7x, 32 devices: a whole 2x2x4 slice. The times are simulated.
32 devices in a mesh: ctx: 2 (over x), head: 4 (over z), roll: 4 (over y, core).
Axes of the slice: x: 2, y: 2, z: 4, core: 2. Of those that a mesh axis runs over, the one named last changes fastest.
Arguments:
- queries: bfloat16 [4, 8, 256, 128], P('roll', 'head', 'ctx'), may hold values from -80 to 80
- cache_keys: bfloat16 [4, 8, 6144, 128], P('roll', 'head', 'ctx'), may hold values from -4.5 to 4.5
- cache_values: bfloat16 [4, 8, 6144, 128], P('roll', 'head', 'ctx'), may hold values from -6 to 6
- new_keys: bfloat16 [4, 8, 16, 128], P('roll', 'head'), may hold values from -12 to 12
- new_values: bfloat16 [4, 8, 16, 128], P('roll', 'head'), may hold values from -6 to 6
- lengths: int32 [4], P('roll'), may hold values from 3072 to 6144, as said below
- positions: int32 [4, 16], P('roll'), may hold values from 3072 to 6159, as said below
- out_weight: bfloat16 [16384, 16384], P('head', ('ctx', 'roll')), may hold values from -0.046875 to 0.046875
Outputs:
- projected: bfloat16 [4, 16, 16384], P('head', None, ('ctx', 'roll'))
Inputs may be any that keep to these rules, and one draw needn't show every extreme that they name: `lengths`: at least one rollout has the full 6144 slots. positions[r] is lengths[r] plus a permutation of 0 .. 15.
All inputs are finite; a program needn't handle non-finite values.
Results may differ from a plain program's by a relative error of at most 0.04.
Values may be sent and summed in bfloat16 or wider, within the bound.
A program may use at most 64 MiB of HBM per device.

v0:
```python
import jax
import jax.numpy as jnp
from jax import lax
from jax.sharding import PartitionSpec as P

NEW = 16
QPK = 16


NEG = -1e30


def shifted(value, axis, steps):
    count = lax.axis_size(axis)
    pairs = [(source, (source + steps) % count) for source in range(count)]
    return lax.ppermute(value, axis, pairs)


def body(queries, cache_keys, cache_values, new_keys, new_values, lengths, positions, out_weight):
    here = lax.axis_index("ctx")
    n_ctx = lax.axis_size("ctx")
    slots = cache_keys.shape[2]
    head_size = cache_keys.shape[3]
    local_heads = cache_keys.shape[1]
    scale = 1.0 / head_size**0.5
    keys = cache_keys[0]
    values = cache_values[0]
    fresh_keys = new_keys[0]
    fresh_values = new_values[0]
    pos = positions[0]
    slot_ok = here * slots + jnp.arange(slots) < lengths[0]

    def update(state, block, first_row, use_new):
        top_old, total_old, summed_old = state
        count = block.shape[1]
        scores = jnp.einsum("krd,ksd->krs", block, keys, preferred_element_type=jnp.float32) * scale
        scores = jnp.where(slot_ok[None, None, :], scores, NEG)
        fresh = (
            jnp.einsum("krd,kud->kru", block, fresh_keys, preferred_element_type=jnp.float32)
            * scale
        )
        token = (first_row + jnp.arange(count)) // QPK
        allow = jnp.logical_and(pos[None, :] <= pos[token][:, None], use_new)
        fresh = jnp.where(allow[None], fresh, NEG)
        top = jnp.maximum(top_old, jnp.maximum(jnp.max(scores, axis=2), jnp.max(fresh, axis=2)))
        cache_weights = jnp.where(
            slot_ok[None, None, :], jnp.exp(scores - top[..., None]), 0.0
        ).astype(jnp.bfloat16)
        fresh_weights = jnp.where(allow[None], jnp.exp(fresh - top[..., None]), 0.0).astype(
            jnp.bfloat16
        )
        factor = jnp.exp(top_old - top)
        total = total_old * factor + jnp.sum(cache_weights.astype(jnp.float32), axis=2)
        total = total + jnp.sum(fresh_weights.astype(jnp.float32), axis=2)
        summed = summed_old * factor[..., None]
        summed = summed + jnp.einsum(
            "krs,ksd->krd", cache_weights, values, preferred_element_type=jnp.float32
        )
        summed = summed + jnp.einsum(
            "kru,kud->krd", fresh_weights, fresh_values, preferred_element_type=jnp.float32
        )
        return (top, total, summed)

    block = queries[0]
    block_rows = block.shape[1]
    state = update(
        (
            jnp.full((local_heads, block_rows), NEG, jnp.float32),
            jnp.zeros((local_heads, block_rows), jnp.float32),
            jnp.zeros((local_heads, block_rows, head_size), jnp.float32),
        ),
        block,
        here * block_rows,
        True,
    )

    def turn(step, carry):
        moving, top, total, summed = carry
        moving = shifted(moving, "ctx", 1)
        top, total, summed = shifted((top, total, summed), "ctx", 1)
        top, total, summed = update((top, total, summed), moving, 0, False)
        return (moving, top, total, summed)

    moving, top, total, summed = lax.fori_loop(
        0, n_ctx - 1, turn, (block, state[0], state[1], state[2])
    )
    attended = (summed / total[..., None]).astype(jnp.bfloat16)
    every = lax.all_gather(attended[None], ("ctx", "roll"), axis=0, tiled=True)
    n_roll = every.shape[0] // n_ctx
    every = every.reshape(n_ctx, n_roll, local_heads, block_rows, head_size)
    every = jnp.roll(every, 1, axis=0)
    rows_all = every.transpose(1, 2, 0, 3, 4).reshape(
        n_roll, local_heads, n_ctx * block_rows, head_size
    )
    n_roll = rows_all.shape[0]
    features = rows_all.reshape(n_roll, local_heads, NEW, QPK, head_size).transpose(0, 2, 1, 3, 4)
    features = features.reshape(n_roll, NEW, local_heads * QPK * head_size)
    return lax.psum_scatter(
        jnp.einsum("rtf,fc->rtc", features, out_weight, preferred_element_type=jnp.float32).astype(
            jnp.bfloat16
        ),
        "head",
        scatter_dimension=0,
        tiled=True,
    )


def solution(mesh):
    in_specs = (
        P("roll", "head", "ctx", None),
        P("roll", "head", "ctx", None),
        P("roll", "head", "ctx", None),
        P("roll", "head", None, None),
        P("roll", "head", None, None),
        P("roll"),
        P("roll", None),
        P("head", ("ctx", "roll")),
    )
    out_specs = P("head", None, ("ctx", "roll"))
    return jax.shard_map(body, mesh=mesh, in_specs=in_specs, out_specs=out_specs, check_vma=False)
```

profile of v0, /device:TPU:0, one launch (start us, length us, event | category | flops | bytes accessed | tf_op | source)
XLA Modules:
  0.0 83.4 jit_solution(11078303917874252622)
XLA Ops:
  6.5 0.0 copy-start
  6.5 0.0 copy-start.1
  6.5 0.0 copy-start.2
  6.5 0.0 copy-start.3
  6.5 0.0 reduce-scatter.2.cloned.1.call-start
  6.6 2.0 %fusion.35 = (s32[1,1]{1,0:T(1,128)}, s32[1,1]{1,0:T(1,128)}, s32[1,1]{1,0:T(1,128)}, s32[1,1]{1,0:T(1,128)}, s32[1,1]{1,0:T(1,128)}, /*index=5*/s32[1,1]{1,0:T(...) fusion(s32[1,16]{1,0:T(1,128)} %param.14), kind=kLoop, calls=%fused_computation.66 | loop fusion | bytes 128 | tf_op jit(solution)/shard_map/gather | solution.py:43
  9.2 10.0 %bitcast_select_fusion.8 = s32[128]{0:T(128)S(1)} fusion(s32[]{:T(128)} %bitcast.22, s32[]{:T(128)} %bitcast.23, s32[]{:T(128)} %bitcast.24, s32[]{:T(128)} %bitcast.25, s32[]{:T(128)} %bitcast.26, s32[]{:T(128)} %bitcast.28, s32[]{:T(128)} %bitcast.27, s32[]{:T(128)} %bitcast.5, s32[]{:T(128)} %bitcast.7, s32[]{:T(128)} %bitcast.9, s32[]{:T(128)} %bitcast.11, ...), kind=kLoop, calls=%fused_computation.42 | loop fusion | flops 6272 | bytes 580 | tf_op jit(solution)/shard_map/gather | solution.py:43
  19.2 0.7 broadcast_compare_fusion
  19.9 1.0 %fusion.37 = (f32[2,128]{1,0:T(2,128)S(1)}, f32[2,128,16]{1,2,0:T(8,128)S(1)}) fusion(bf16[1,2,16,128]{3,2,1,0:T(8,128)(2,1)} %param.11, bf16[1,2,128,128]{3,2,1,0:T(8,128)(2,1)} %param.8, pred[128,16]{0,1:T(8,128)(4,1)S(1)} %broadcast_compare_fusion), kind=kOutput, calls=%fused_computation.68 | convolution fusion | flops 1060608 | bytes 93184 | tf_op jit(solution)/shard_map/krd,kud->kru/dot_general | solution.py:39
  20.9 0.0 copy-done
  20.9 1.5 %fusion.36 = (f32[2,128]{1,0:T(2,128)S(1)}, f32[2,128,3072]{2,1,0:T(8,128)S(1)}) fusion(bf16[1,2,3072,128]{3,2,1,0:T(8,128)(2,1)S(1)} %copy-done, bf16[1,2,128,128]{3,2,1,0:T(8,128)(2,1)} %param.8, pred[3072]{0:T(1024)(128)(4,1)S(1)} %add_compare_fusion), kind=kOutput, calls=%fused_computation.67 | convolution fusion | flops 203685632 | bytes 4788224 | tf_op jit(solution)/shard_map/krd,ksd->krs/dot_general | solution.py:36
  22.4 3.0 %collective-permute-start.1 = (f32[2,128]{1,0:T(2,128)S(1)}, f32[2,128]{1,0:T(2,128)S(1)}, u32[]{:S(2)}, u32[]{:S(2)}) collective-permute-start(f32[2,128]{1,0:T(2,128)S(1)} %get-tuple-element.28), channel_id=1, source_target_pairs={{0,16},{16,0},{1,17},{17,1},{2,18},{18,2},{3,19},{19,3},{4,20},{20... | collective-permute-start | bytes 3080 | tf_op jit(solution)/shard_map/while/body/eval_jaxpr/ppermute | solution.py:16
  25.4 0.0 copy-done.1
  25.5 0.1 collective-permute-start.2
  25.5 0.0 copy-done.2
  25.5 0.2 fusion.22
  25.8 0.0 copy-done.3
  25.8 0.7 fusion.16
  26.5 2.0 %collective-permute-start = (f32[2,128,128]{2,1,0:T(8,128)S(1)}, f32[2,128,128]{2,1,0:T(8,128)S(1)}, u32[]{:S(2)}, u32[]{:S(2)}) collective-permute-start(f32[2,128,128]{2,1,0:T(8,128)S(1)} %fusion.16), channel_id=1, source_target_pairs={{0,16},{16,0},{1,17},{17,1},{2,18},{18,2},{3,19},{19,3},{4,20},{20... | collective-permute-start | bytes 393224 | tf_op jit(solution)/shard_map/while/body/eval_jaxpr/ppermute | solution.py:16
  28.5 1.9 %collective-permute-done.2 = bf16[2,128,128]{2,1,0:T(8,128)(2,1)S(1)} collective-permute-done((bf16[2,128,128]{2,1,0:T(8,128)(2,1)S(1)}, bf16[2,128,128]{2,1,0:T(8,128)(2,1)S(1)}, u32[]{:S(2)}, u32[]{:S(2)}) %collective-permute-start.2) | collective-permute-done | bytes 65568 | tf_op jit(solution)/shard_map/while/body/eval_jaxpr/ppermute | solution.py:16
  30.4 0.7 fusion.38
  31.1 0.0 collective-permute-done.1
  31.1 1.2 %convert_reduce_fusion.1 = (f32[2,128]{1,0:T(2,128)S(1)}, f32[2,128]{1,0:T(2,128)S(1)}) fusion(f32[2,128,3072]{2,1,0:T(8,128)S(1)} %get-tuple-element.60, f32[2,128]{1,0:T(2,128)S(1)} %get-tuple-element.28, pred[3072]{0:T(1024)(128)(4,1)S(1)} %add_compare_fusion, f32[2,128,3072]{2,1,0:T(8,128)S(1)} %get-tuple-element.64, f32[2,128]{1,0:T(2,128)S(1)} %maximum_maximum_fusion), kind=kLoop, calls=%fused_computation.7 | loop fusion | flops 7863808 | bytes 6298624 | tf_op jit(solution)/shard_map/reduce_sum | solution.py:53
  32.4 0.1 collective-permute-start.3
  32.4 0.1 fusion.20
  32.6 3.4 %collective-permute-done.3 = f32[2,128]{1,0:T(2,128)S(1)} collective-permute-done((f32[2,128]{1,0:T(2,128)S(1)}, f32[2,128]{1,0:T(2,128)S(1)}, u32[]{:S(2)}, u32[]{:S(2)}) %collective-permute-start.3) | collective-permute-done | bytes 1056 | tf_op jit(solution)/shard_map/while/body/eval_jaxpr/ppermute | solution.py:16
  36.0 0.0 collective-permute-done
  36.0 0.7 divide_convert_fusion
  36.8 9.9 %all-gather = bf16[16,128,128]{2,1,0:T(8,128)(2,1)S(1)} all-gather(bf16[2,128,128]{2,1,0:T(8,128)(2,1)S(1)} %divide_convert_fusion), channel_id=2, replica_groups=mesh['ctx'=2,'head'=4,'roll'=4] {'ctx','roll'}, dimensions={0}, use_global_device_ids=true | all-gather | bytes 589824 | tf_op jit(solution)/shard_map/all_gather | solution.py:88
  46.7 0.1 pad_maximum_fusion
  46.8 0.2 reshape.115
  47.0 9.5 %fusion.4 = bf16[4,16,2048]{2,1,0:T(8,128)(2,1)} fusion(bf16[4,16,4096]{2,1,0:T(8,128)(2,1)S(1)} %reshape.115, bf16[4096,2048]{1,0:T(8,128)(2,1)} %param.15), kind=kOutput, calls=%fused_computation.10 | convolution fusion | flops 1073872896 | bytes 17563648 | tf_op jit(solution)/shard_map/rtf,fc->rtc/dot_general | solution.py:99
  56.5 0.0 reduce-scatter.2.cloned.1.call-update
  56.5 20.0 %reduce-scatter.2.cloned.1.call-done = bf16[1,16,2048]{2,1,0:T(8,128)(2,1)} async-done(((bf16[4,16,2048]{2,1,0:T(8,128)(2,1)}), bf16[1,16,2048]{2,1,0:T(8,128)(2,1)}) %reduce-scatter.2.cloned.1.call-update) | async-done | bytes 65552 | tf_op jit(solution)/shard_map/reduce_scatter | solution.py:98
  (8 shorter events, 0.1 us)
Async XLA Ops:
  6.5 14.4 %copy-start = (bf16[1,2,3072,128]{3,2,1,0:T(8,128)(2,1)S(1)}, bf16[1,2,3072,128]{3,2,1,0:T(8,128)(2,1)}, u32[]{:S(2)}) copy-start(bf16[1,2,3072,128]{3,2,1,0:T(8,128)(2,1)} %param.9) | copy-start | bytes 4718596
  6.5 18.9 %copy-start.1 = (bf16[1,2,128,128]{3,2,1,0:T(8,128)(2,1)S(1)}, bf16[1,2,128,128]{3,2,1,0:T(8,128)(2,1)}, u32[]{:S(2)}) copy-start(bf16[1,2,128,128]{3,2,1,0:T(8,128)(2,1)} %param.8) | copy-start | bytes 196612
  6.5 19.0 %copy-start.2 = (bf16[1,2,16,128]{3,2,1,0:T(8,128)(2,1)S(1)}, bf16[1,2,16,128]{3,2,1,0:T(8,128)(2,1)}, u32[]{:S(2)}) copy-start(bf16[1,2,16,128]{3,2,1,0:T(8,128)(2,1)} %param.12) | copy-start | bytes 24580
  6.5 19.2 %copy-start.3 = (bf16[1,2,3072,128]{3,2,1,0:T(8,128)(2,1)S(1)}, bf16[1,2,3072,128]{3,2,1,0:T(8,128)(2,1)}, u32[]{:S(2)}) copy-start(bf16[1,2,3072,128]{3,2,1,0:T(8,128)(2,1)} %param.10) | copy-start | bytes 4718596
  6.5 70.0 %reduce-scatter.2.cloned.1.call-start = ((), (), s32[]{:S(2)}) async-start(), calls=%async_computation.1 | async-start | bytes 327680 | tf_op jit(solution)/shard_map/reduce_scatter | solution.py:98
  22.4 8.6 %collective-permute-start.1 = (f32[2,128]{1,0:T(2,128)S(1)}, f32[2,128]{1,0:T(2,128)S(1)}, u32[]{:S(2)}, u32[]{:S(2)}) collective-permute-start(f32[2,128]{1,0:T(2,128)S(1)} %get-tuple-element.28), channel_id=1, source_target_pairs={{0,16},{16,0},{1,17},{17,1},{2,18},{18,2},{3,19},{19,3},{4,20},{20... | collective-permute-start | bytes 3080 | tf_op jit(solution)/shard_map/while/body/eval_jaxpr/ppermute | solution.py:16
  25.5 5.0 %collective-permute-start.2 = (bf16[2,128,128]{2,1,0:T(8,128)(2,1)S(1)}, bf16[2,128,128]{2,1,0:T(8,128)(2,1)S(1)}, u32[]{:S(2)}, u32[]{:S(2)}) collective-permute-start(bf16[2,128,128]{2,1,0:T(8,128)(2,1)S(1)} %bitcast.115), channel_id=1, source_target_pairs={{0,16},{16,0},{1,17},{17,1},{2,18},{18,2},{3,19},{19,3},{4,20},{20... | collective-permute-start | bytes 196616 | tf_op jit(solution)/shard_map/while/body/eval_jaxpr/ppermute | solution.py:16
  26.5 9.5 %collective-permute-start = (f32[2,128,128]{2,1,0:T(8,128)S(1)}, f32[2,128,128]{2,1,0:T(8,128)S(1)}, u32[]{:S(2)}, u32[]{:S(2)}) collective-permute-start(f32[2,128,128]{2,1,0:T(8,128)S(1)} %fusion.16), channel_id=1, source_target_pairs={{0,16},{16,0},{1,17},{17,1},{2,18},{18,2},{3,19},{19,3},{4,20},{20... | collective-permute-start | bytes 393224 | tf_op jit(solution)/shard_map/while/body/eval_jaxpr/ppermute | solution.py:16
  32.4 3.6 %collective-permute-start.3 = (f32[2,128]{1,0:T(2,128)S(1)}, f32[2,128]{1,0:T(2,128)S(1)}, u32[]{:S(2)}, u32[]{:S(2)}) collective-permute-start(f32[2,128]{1,0:T(2,128)S(1)} %add_add_fusion), channel_id=1, source_target_pairs={{0,16},{16,0},{1,17},{17,1},{2,18},{18,2},{3,19},{19,3},{4,20},{20... | collective-permute-start | bytes 3080 | tf_op jit(solution)/shard_map/while/body/eval_jaxpr/ppermute | solution.py:16
Sparse Core Ops, SparseCore 0:
  56.6 19.8 reduce-scatter.1
where the time goes:
time: 83.8 us; the launch traced here: 83.4 us
  waiting for transfers between devices  25.3 us (30%)
  matrix products  14.5 us (17%)
  between operations  14.2 us (17%)
  other arithmetic  12 us (14%)
  blocking collectives  9.87 us (12%)
  starting transfers between devices  5.2 us (6%)
  local copies, waits for them, and re-layouts  2.27 us (3%)
    reduce_scatter x1, waiting for transfers between devices, body(): lax.psum_scatter(jnp.einsum('rtf,fc->rtc', features, out_weight, preferre...  20 us
    gather x1, other arithmetic, update(): allow = jnp.logical_and(pos[None, :] <= pos[token][:, None], use_new)  9.96 us
    all_gather x1, blocking collectives, body(): every = lax.all_gather(attended[None], ('ctx', 'roll'), axis=0, tiled=True)  9.87 us
    dot_general x1, matrix products, body(): jnp.einsum('rtf,fc->rtc', features, out_weight, preferred_element_type=jn...  9.49 us
    ppermute x4, waiting for transfers between devices, shifted(): return lax.ppermute(value, axis, pairs)  5.31 us
    ppermute x4, starting transfers between devices, shifted(): return lax.ppermute(value, axis, pairs)  5.17 us
    dot_general x2, matrix products, update(): jnp.einsum('krd,ksd->krs', block, keys, preferred_element_type=jnp.float32)  2.18 us
    gather x1, local copies, waits for them, and re-layouts, update(): allow = jnp.logical_and(pos[None, :] <= pos[token][:, None], use_new)  1.95 us
  transfers between devices with their start and end apart: 5, of which 3 were waited for; matrix products, arithmetic and copies ran while one was open for 4% of the time, Pallas kernels for 0%

commit v1 on v0

--- a/solution.py
+++ b/solution.py
@@ -1,6 +1,11 @@
+import functools
+import math
+
 import jax
 import jax.numpy as jnp
 from jax import lax
+from jax.experimental import pallas as pl
+from jax.experimental.pallas import tpu as pltpu
 from jax.sharding import PartitionSpec as P
 
 NEW = 16
@@ -8,6 +13,316 @@
 
 
 NEG = -1e30
+
+MESH = pl.DeviceIdType.MESH
+CHUNK = 512
+COLS = 512
+WCUT = 4
+
+
+def fused_kernel(
+    n_head,
+    q_hbm, k_hbm, v_hbm, fk_hbm, fv_hbm, len_ref, pos_ref, w_hbm,
+    out_ref,
+    qbuf, kbuf, vbuf, fkbuf, fvbuf, wbuf, sbuf,
+    po_send, po_recv, st_send, st_recv, fbuf, gather, accbuf, rs_send, rs_recv,
+    q_sem, k_sem, v_sem, f_sem, w_sem,
+    qx_send, qx_recv, px_send, px_recv, sx_send, sx_recv,
+    g_send, g_recv, rs_send_sem, rs_recv_sem,
+):
+    f32, bf16 = jnp.float32, jnp.bfloat16
+    c, h, r = lax.axis_index("ctx"), lax.axis_index("head"), lax.axis_index("roll")
+    other = 1 - c
+    sib = r + 1 - 2 * lax.rem(r, 2)
+    far = lax.rem(r + 2, 4)
+    far_sib = lax.rem(sib + 2, 4)
+    partner = {"ctx": other}
+    rows, head_size = qbuf.shape[1], qbuf.shape[2]
+    half = rows // 2
+    slots = kbuf.shape[1]
+    factor = math.log2(math.e) / math.sqrt(head_size)
+
+    barrier = pltpu.get_barrier_semaphore()
+    peers = [partner, {"roll": sib}, {"roll": far}, {"ctx": other, "roll": far}]
+    peers += [{"head": lax.rem(h + off, n_head)} for off in range(1, n_head)]
+    for peer in peers:
+        pl.semaphore_signal(barrier, inc=1, device_id=peer, device_id_type=MESH)
+
+    local = {}
+
+    def fetch(name, src, dst, sem):
+        local[name] = pltpu.make_async_copy(src, dst, sem)
+        local[name].start()
+
+    mine = pl.ds(pl.multiple_of(c * half, half), half)
+    fetch("q", q_hbm.at[0], qbuf.at[:, mine, :], q_sem)
+    fetch("k0", k_hbm.at[0, other], kbuf.at[other], k_sem.at[0])
+    fetch("v0", v_hbm.at[0, other], vbuf.at[other], v_sem.at[0])
+    fetch("k1", k_hbm.at[0, c], kbuf.at[c], k_sem.at[1])
+    fetch("v1", v_hbm.at[0, c], vbuf.at[c], v_sem.at[1])
+    fetch("fk", fk_hbm.at[0, c], fkbuf, f_sem.at[0])
+    fetch("fv", fv_hbm.at[0, c], fvbuf, f_sem.at[1])
+
+    pl.semaphore_wait(barrier, len(peers))
+
+    q_copies = []
+    for at, head in enumerate((c, other)):
+        q_copies.append(
+            pltpu.make_async_remote_copy(
+                src_ref=q_hbm.at[0, head],
+                dst_ref=qbuf.at[head, mine, :],
+                send_sem=qx_send.at[at],
+                recv_sem=qx_recv.at[at],
+                device_id=partner,
+                device_id_type=MESH,
+            )
+        )
+        q_copies[-1].start()
+
+    depth = w_hbm.shape[0] // 2
+    piece = depth // WCUT
+    for at, head in enumerate((c, other)):
+        for cut in range(WCUT):
+            fetch(
+                ("w", at, cut),
+                w_hbm.at[pl.ds(pl.multiple_of(head * depth + cut * piece, piece), piece), :],
+                wbuf.at[head, pl.ds(cut * piece, piece), :],
+                w_sem.at[at, cut],
+            )
+
+    length = len_ref[0]
+    first_slot = c * slots
+
+    def scores(query, head):
+        fold = jnp.full((query.shape[0], 128), NEG, f32)
+        for at in range(slots // CHUNK):
+            span = slice(at * CHUNK, (at + 1) * CHUNK)
+            part = lax.dot_general(
+                query, kbuf[head, span, :], (((1,), (1,)), ((), ())), preferred_element_type=f32
+            )
+            slot = first_slot + at * CHUNK + lax.broadcasted_iota(jnp.int32, (1, CHUNK), 1)
+            part = part + jnp.where(slot < length, 0.0, NEG)
+            sbuf[0 : query.shape[0], span] = part
+            for lane in range(CHUNK // 128):
+                fold = jnp.maximum(fold, part[:, lane * 128 : (lane + 1) * 128])
+        return jnp.max(fold, axis=1, keepdims=True)
+
+    def weighted(count, head, top):
+        ones = jnp.ones((CHUNK, 128), bf16)
+        acc = jnp.zeros((count, head_size + 128), f32)
+        for at in range(slots // CHUNK):
+            span = slice(at * CHUNK, (at + 1) * CHUNK)
+            weights = jnp.exp2((sbuf[0:count, span] - top) * factor).astype(bf16)
+            both = jnp.concatenate([vbuf[head, span, :], ones], axis=1)
+            acc = acc + jnp.dot(weights, both, preferred_element_type=f32)
+        return acc[:, :head_size], acc[:, head_size:]
+
+    lane = lax.broadcasted_iota(jnp.int32, (half, 128), 1)
+    p_copies, s_copies = [], []
+    for at, side in enumerate((c, other)):
+        if at == 0:
+            local["q"].wait()
+            local["k0"].wait()
+        else:
+            q_copies[0].wait_recv()
+        query = qbuf[other, pl.ds(pl.multiple_of(side * half, half), half), :]
+        top = scores(query, other)
+        if at == 0:
+            local["v0"].wait()
+        summed, total = weighted(half, other, top)
+        po_send[side] = summed.astype(bf16)
+        turned = jnp.transpose(jnp.where(lane < 64, jnp.broadcast_to(top, (half, 128)), total))
+        st_send[side, 0:8, :] = turned[0:8, :]
+        st_send[side, 8:16, :] = turned[64:72, :]
+        p_copies.append(
+            pltpu.make_async_remote_copy(
+                src_ref=po_send.at[side], dst_ref=po_recv.at[side],
+                send_sem=px_send.at[at], recv_sem=px_recv.at[at],
+                device_id=partner, device_id_type=MESH,
+            )
+        )
+        s_copies.append(
+            pltpu.make_async_remote_copy(
+                src_ref=st_send.at[side], dst_ref=st_recv.at[side],
+                send_sem=sx_send.at[at], recv_sem=sx_recv.at[at],
+                device_id=partner, device_id_type=MESH,
+            )
+        )
+        p_copies[-1].start()
+        s_copies[-1].start()
+
+    token = lax.broadcasted_iota(jnp.int32, (rows, NEW), 0) // QPK
+    fresh_at = lax.broadcasted_iota(jnp.int32, (rows, NEW), 1)
+    row_pos = jnp.zeros((rows, NEW), jnp.int32)
+    new_pos = jnp.zeros((rows, NEW), jnp.int32)
+    for t in range(NEW):
+        value = pos_ref[0, t]
+        row_pos = jnp.where(token == t, value, row_pos)
+        new_pos = jnp.where(fresh_at == t, value, new_pos)
+    allow = new_pos <= row_pos
+
+    q_copies[1].wait_recv()
+    local["k1"].wait()
+    local["fk"].wait()
+    query = qbuf[c]
+    top = scores(query, c)
+    fresh = lax.dot_general(
+        query, fkbuf[...], (((1,), (1,)), ((), ())), preferred_element_type=f32
+    )
+    fresh = jnp.where(allow, fresh, NEG)
+    top = jnp.maximum(top, jnp.max(fresh, axis=1, keepdims=True))
+    local["v1"].wait()
+    local["fv"].wait()
+    summed, total = weighted(rows, c, top)
+    fresh_weights = jnp.where(allow, jnp.exp2((fresh - top) * factor), 0.0).astype(bf16)
+    summed = summed + jnp.dot(fresh_weights, fvbuf[...], preferred_element_type=f32)
+    total = total + jnp.sum(fresh_weights.astype(f32), axis=1, keepdims=True)
+
+    for copy in p_copies + s_copies:
+        copy.wait_recv()
+    for side in range(2):
+        span = slice(side * half, (side + 1) * half)
+        top_here = jnp.broadcast_to(top[span], (half, 128))
+        top_there = jnp.transpose(jnp.broadcast_to(st_recv[side, 0:1, :], (128, half)))
+        total_there = jnp.transpose(jnp.broadcast_to(st_recv[side, 8:9, :], (128, half)))
+        best = jnp.maximum(top_here, top_there)
+        here = jnp.exp2((top_here - best) * factor)
+        there = jnp.exp2((top_there - best) * factor)
+        num = summed[span] * here + po_recv[side].astype(f32) * there
+        den = total[span] * here + total_there * there
+        fbuf[span, :] = num / den
+    for j in range(QPK):
+        feature = fbuf[pl.ds(j, NEW, stride=QPK), :]
+        gather[c, r, :, j * head_size : (j + 1) * head_size] = feature.astype(bf16)
+
+    def pass_on(at, slot_c, slot_r, peer):
+        block = gather.at[slot_c, slot_r]
+        copy = pltpu.make_async_remote_copy(
+            src_ref=block, dst_ref=block,
+            send_sem=g_send.at[at], recv_sem=g_recv.at[at],
+            device_id=peer, device_id_type=MESH,
+        )
+        copy.start()
+        return copy
+
+    g_far = pass_on(0, c, r, {"roll": far})
+    g_sib = pass_on(1, c, r, {"roll": sib})
+    g_ctx = pass_on(2, c, r, partner)
+    g_diag = pass_on(3, c, r, {"ctx": other, "roll": far})
+    g_far.wait_recv()
+    f_far = pass_on(4, c, far, {"roll": sib})
+    for at in range(2):
+        for cut in range(WCUT):
+            local[("w", at, cut)].wait()
+    g_sib.wait_recv()
+    f_far.wait_recv()
+
+    n_cols = wbuf.shape[2] // COLS
+    tokens = gather.shape[1] * NEW
+
+    def project(head, at):
+        features = gather[head].reshape(tokens, depth)
+        return jnp.dot(
+            features, wbuf[head, :, at * COLS : (at + 1) * COLS], preferred_element_type=f32
+        )
+
+    f_ctx = f_diag = None
+    for at in range(n_cols):
+        accbuf[:, at * COLS : (at + 1) * COLS] = project(c, at)
+        if at == n_cols // 2 - 1:
+            g_ctx.wait_recv()
+            f_ctx = pass_on(5, other, r, {"roll": sib})
+        if at == n_cols - 2:
+            g_diag.wait_recv()
+            f_diag = pass_on(6, other, far, {"roll": sib})
+    f_ctx.wait_recv()
+    f_diag.wait_recv()
+
+    rs_copies = []
+    for at in range(n_cols):
+        span = slice(at * COLS, (at + 1) * COLS)
+        part = accbuf[:, span] + project(other, at)
+        accbuf[:, span] = part
+        rs_send[:, :, span] = part.astype(bf16).reshape(n_head, NEW, COLS)
+        for off in range(n_head - 1, 0, -1):
+            to = lax.rem(h + off, n_head)
+            copy = pltpu.make_async_remote_copy(
+                src_ref=rs_send.at[to, :, span],
+                dst_ref=rs_recv.at[off - 1, :, span],
+                send_sem=rs_send_sem.at[off - 1, at],
+                recv_sem=rs_recv_sem.at[off - 1, at],
+                device_id={"head": to},
+                device_id_type=MESH,
+            )
+            copy.start()
+            rs_copies.append((at, copy))
+
+    own = pl.ds(pl.multiple_of(h * NEW, NEW), NEW)
+    for at in range(n_cols):
+        span = slice(at * COLS, (at + 1) * COLS)
+        for place, copy in rs_copies:
+            if place == at:
+                copy.wait_recv()
+        value = accbuf[own, span]
+        for off in range(n_head - 1):
+            value = value + rs_recv[off, :, span].astype(f32)
+        out_ref[0, :, span] = value.astype(bf16)
+
+    for copy in q_copies + p_copies + s_copies:
+        copy.wait_send()
+    for copy in (g_far, g_sib, g_ctx, g_diag, f_far, f_ctx, f_diag):
+        copy.wait_send()
+    for _, copy in rs_copies:
+        copy.wait_send()
+
+
+def fused_body(n_head, queries, cache_keys, cache_values, new_keys, new_values, lengths, positions, out_weight):
+    f32, bf16 = jnp.float32, jnp.bfloat16
+    _, heads, slots, head_size = cache_keys.shape
+    half = queries.shape[2]
+    rows = 2 * half
+    width = out_weight.shape[1]
+    depth = out_weight.shape[0] // heads
+    n_cols = width // COLS
+    dma = pltpu.SemaphoreType.DMA
+    anywhere = pl.BlockSpec(memory_space=pl.ANY)
+    scalars = pl.BlockSpec(memory_space=pltpu.SMEM)
+    return pl.pallas_call(
+        functools.partial(fused_kernel, n_head),
+        out_shape=jax.ShapeDtypeStruct((1, NEW, width), bf16),
+        in_specs=[anywhere] * 5 + [scalars] * 2 + [anywhere],
+        out_specs=pl.BlockSpec(memory_space=pltpu.VMEM),
+        scratch_shapes=[
+            pltpu.VMEM((heads, rows, head_size), bf16),
+            pltpu.VMEM((heads, slots, head_size), bf16),
+            pltpu.VMEM((heads, slots, head_size), bf16),
+            pltpu.VMEM((NEW, head_size), bf16),
+            pltpu.VMEM((NEW, head_size), bf16),
+            pltpu.VMEM((heads, depth, width), bf16),
+            pltpu.VMEM((rows, slots), f32),
+            pltpu.VMEM((2, half, head_size), bf16),
+            pltpu.VMEM((2, half, head_size), bf16),
+            pltpu.VMEM((2, 16, half), f32),
+            pltpu.VMEM((2, 16, half), f32),
+            pltpu.VMEM((rows, head_size), f32),
+            pltpu.VMEM((2, 4, NEW, depth), bf16),
+            pltpu.VMEM((4 * NEW, width), f32),
+            pltpu.VMEM((n_head, NEW, width), bf16),
+            pltpu.VMEM((n_head - 1, NEW, width), bf16),
+            dma, dma((2,)), dma((2,)), dma((2,)), dma((2, WCUT)),
+            dma((2,)), dma((2,)), dma((2,)), dma((2,)), dma((2,)), dma((2,)),
+            dma((7,)), dma((7,)),
+            dma((n_head - 1, n_cols)), dma((n_head - 1, n_cols)),
+        ],
+        compiler_params=pltpu.CompilerParams(
+            collective_id=0, has_side_effects=True, vmem_limit_bytes=48 * 1024 * 1024
+        ),
+        cost_estimate=pl.CostEstimate(
+            flops=4 * heads * rows * slots * head_size + 2 * 4 * NEW * heads * depth * width,
+            bytes_accessed=2 * heads * (2 * slots * head_size + depth * width),
+            transcendentals=heads * rows * slots,
+        ),
+    )(queries, cache_keys, cache_values, new_keys, new_values, lengths, positions, out_weight)
 
 
 def shifted(value, axis, steps):
@@ -16,7 +331,7 @@
     return lax.ppermute(value, axis, pairs)
 
 
-def body(queries, cache_keys, cache_values, new_keys, new_values, lengths, positions, out_weight):
+def ring_body(queries, cache_keys, cache_values, new_keys, new_values, lengths, positions, out_weight):
     here = lax.axis_index("ctx")
     n_ctx = lax.axis_size("ctx")
     slots = cache_keys.shape[2]
@@ -117,4 +432,7 @@
         P("head", ("ctx", "roll")),
     )
     out_specs = P("head", None, ("ctx", "roll"))
+    body = ring_body
+    if (mesh.shape["ctx"], mesh.shape["head"], mesh.shape["roll"]) == (2, 4, 4):
+        body = functools.partial(fused_body, mesh.shape["head"])
     return jax.shard_map(body, mesh=mesh, in_specs=in_specs, out_specs=out_specs, check_vma=False)

time: 83.8 us -> 36.2 us (0.43)
  Pallas kernels: 0 us -> 28.9 us
  waiting for transfers between devices: 25.3 us -> 0 us
  matrix products: 14.5 us -> 0 us
  between operations: 14.2 us -> 0.67 us
  other arithmetic: 12 us -> 0 us
  blocking collectives: 9.87 us -> 0 us
  starting transfers between devices: 5.2 us -> 0 us
  local copies, waits for them, and re-layouts: 2.27 us -> 6.33 us
    pallas_call x0 -> x1, Pallas kernels: none -> 28.9 us  [fused_body(): pl.pallas_call(functools.partial(fused_kernel, n_head), out_shape=jax.Sha...]
    reduce_scatter x1 -> x0, waiting for transfers between devices: 20 us -> none  [body(): lax.psum_scatter(jnp.einsum('rtf,fc->rtc', features, out_weight, preferre...]
    dot_general x8 -> x0, matrix products: 14.5 us -> none  [the longest x1 9.49 us: body(): jnp.einsum('rtf,fc->rtc', features, out_weight, preferred_element_type=jn...]
    gather x1 -> x0, other arithmetic: 9.96 us -> none  [update(): allow = jnp.logical_and(pos[None, :] <= pos[token][:, None], use_new)]
    all_gather x1 -> x0, blocking collectives: 9.87 us -> none  [body(): every = lax.all_gather(attended[None], ('ctx', 'roll'), axis=0, tiled=True)]
    unnamed x8 -> x13, local copies, waits for them, and re-layouts: 0.02 us -> 6.33 us
    ppermute x4 -> x0, waiting for transfers between devices: 5.31 us -> none  [shifted(): return lax.ppermute(value, axis, pairs)]
    ppermute x4 -> x0, starting transfers between devices: 5.17 us -> none  [shifted(): return lax.ppermute(value, axis, pairs)]
  transfers between devices with their start and end apart: 5 -> 0, of which waited for: 3 -> 0; matrix products, arithmetic and copies ran while one was open for 4% -> 0% of each run, Pallas kernels for 0% -> 0%
where the time goes in v1:
time: 36.2 us; the launch traced here: 35.9 us
  Pallas kernels  28.9 us (80%)
  local copies, waits for them, and re-layouts  6.33 us (17%)
  between operations  0.67 us (2%)
    pallas_call x1, Pallas kernels, fused_body(): pl.pallas_call(functools.partial(fused_kernel, n_head), out_shape=jax.Sha...  28.9 us
    unnamed x13, local copies, waits for them, and re-layouts  6.33 us

profile of v1, /device:TPU:0, one launch (start us, length us, event | category | flops | bytes accessed | tf_op | source)
XLA Modules:
  0.0 35.9 jit_solution(9312129066238434964)
XLA Ops:
  0.7 0.0 copy-start
  0.7 1.4 %copy-done = bf16[1,2,3072,128]{3,2,1,0:T(8,128)(2,1)S(1)} copy-done((bf16[1,2,3072,128]{3,2,1,0:T(8,128)(2,1)S(1)}, bf16[1,2,3072,128]{3,2,1,0:T(8,128)(2,1)}, u32[]{:S(2)}) %copy-start) | copy-done | bytes 1572888
  2.1 0.0 copy-start.1
  2.1 1.4 %copy-done.1 = bf16[1,2,3072,128]{3,2,1,0:T(8,128)(2,1)S(1)} copy-done((bf16[1,2,3072,128]{3,2,1,0:T(8,128)(2,1)S(1)}, bf16[1,2,3072,128]{3,2,1,0:T(8,128)(2,1)}, u32[]{:S(2)}) %copy-start.1) | copy-done | bytes 1572888
  3.5 0.0 copy-start.2
  3.5 0.8 %copy-done.2 = bf16[1,2,128,128]{3,2,1,0:T(8,128)(2,1)S(1)} copy-done((bf16[1,2,128,128]{3,2,1,0:T(8,128)(2,1)S(1)}, bf16[1,2,128,128]{3,2,1,0:T(8,128)(2,1)}, u32[]{:S(2)}) %copy-start.2) | copy-done | bytes 65560
  4.3 0.0 copy-start.3
  4.3 0.7 %copy-done.3 = bf16[1,2,16,128]{3,2,1,0:T(8,128)(2,1)S(1)} copy-done((bf16[1,2,16,128]{3,2,1,0:T(8,128)(2,1)S(1)}, bf16[1,2,16,128]{3,2,1,0:T(8,128)(2,1)}, u32[]{:S(2)}) %copy-start.3) | copy-done | bytes 8216
  5.0 0.0 copy-start.4
  5.0 0.7 %copy-done.4 = bf16[1,2,16,128]{3,2,1,0:T(8,128)(2,1)S(1)} copy-done((bf16[1,2,16,128]{3,2,1,0:T(8,128)(2,1)S(1)}, bf16[1,2,16,128]{3,2,1,0:T(8,128)(2,1)}, u32[]{:S(2)}) %copy-start.4) | copy-done | bytes 8216
  5.7 0.0 copy-start.5
  5.7 0.7 %copy-done.5 = s32[1,16]{1,0:T(1,128)S(1)} copy-done((s32[1,16]{1,0:T(1,128)S(1)}, s32[1,16]{1,0:T(1,128)}, u32[]{:S(2)}) %copy-start.5) | copy-done | bytes 88
  6.4 28.9 %shard_map.82 = bf16[1,16,2048]{2,1,0:T(8,128)(2,1)S(1)} custom-call(bf16[1,2,128,128]{3,2,1,0:T(8,128)(2,1)S(1)} %copy-done.2, bf16[1,2,3072,128]{3,2,1,0:T(8,128)(2,1)S(1)} %copy-done, bf16[1,2,3072,128]{3,2,1,0:T(8,128)(2,1)S(1)} %copy-done.1, bf16[1,2,16,128]{3,2,1,0:T(8,128)(2,1)S(1)} %copy-done.3, bf16[1,2,16,128]{3,2,1,0:T(8,128)(2,1)S(1)} %copy-done.4, ...), custom_call_target="tpu_custom_call" | custom-call | flops 1879048192 | bytes 19922944 | tf_op jit(solution)/shard_map/pallas_call | solution.py:290
  35.3 0.6 %copy.11 = bf16[1,16,2048]{2,1,0:T(8,128)(2,1)} copy(bf16[1,16,2048]{2,1,0:T(8,128)(2,1)S(1)} %shard_map.82) | data formatting | bytes 131072
Async XLA Ops:
  0.7 1.4 %copy-start = (bf16[1,2,3072,128]{3,2,1,0:T(8,128)(2,1)S(1)}, bf16[1,2,3072,128]{3,2,1,0:T(8,128)(2,1)}, u32[]{:S(2)}) copy-start(bf16[1,2,3072,128]{3,2,1,0:T(8,128)(2,1)} %k_hbm.1) | copy-start | bytes 4718596
  2.1 1.4 %copy-start.1 = (bf16[1,2,3072,128]{3,2,1,0:T(8,128)(2,1)S(1)}, bf16[1,2,3072,128]{3,2,1,0:T(8,128)(2,1)}, u32[]{:S(2)}) copy-start(bf16[1,2,3072,128]{3,2,1,0:T(8,128)(2,1)} %v_hbm.1) | copy-start | bytes 4718596
  3.5 0.8 %copy-start.2 = (bf16[1,2,128,128]{3,2,1,0:T(8,128)(2,1)S(1)}, bf16[1,2,128,128]{3,2,1,0:T(8,128)(2,1)}, u32[]{:S(2)}) copy-start(bf16[1,2,128,128]{3,2,1,0:T(8,128)(2,1)} %q_hbm.1) | copy-start | bytes 196612
  4.3 0.7 %copy-start.3 = (bf16[1,2,16,128]{3,2,1,0:T(8,128)(2,1)S(1)}, bf16[1,2,16,128]{3,2,1,0:T(8,128)(2,1)}, u32[]{:S(2)}) copy-start(bf16[1,2,16,128]{3,2,1,0:T(8,128)(2,1)} %fk_hbm.1) | copy-start | bytes 24580
  5.0 0.7 %copy-start.4 = (bf16[1,2,16,128]{3,2,1,0:T(8,128)(2,1)S(1)}, bf16[1,2,16,128]{3,2,1,0:T(8,128)(2,1)}, u32[]{:S(2)}) copy-start(bf16[1,2,16,128]{3,2,1,0:T(8,128)(2,1)} %fv_hbm.1) | copy-start | bytes 24580
  5.7 0.7 %copy-start.5 = (s32[1,16]{1,0:T(1,128)S(1)}, s32[1,16]{1,0:T(1,128)}, u32[]{:S(2)}) copy-start(s32[1,16]{1,0:T(1,128)} %pos_ref.1) | copy-start | bytes 196

commit v2 on v1

--- a/solution.py
+++ b/solution.py
@@ -119,12 +119,8 @@
 
     lane = lax.broadcasted_iota(jnp.int32, (half, 128), 1)
     p_copies, s_copies = [], []
-    for at, side in enumerate((c, other)):
-        if at == 0:
-            local["q"].wait()
-            local["k0"].wait()
-        else:
-            q_copies[0].wait_recv()
+
+    def give_back(at, side):
         query = qbuf[other, pl.ds(pl.multiple_of(side * half, half), half), :]
         top = scores(query, other)
         if at == 0:
@@ -148,49 +144,65 @@
                 device_id=partner, device_id_type=MESH,
             )
         )
+        s_copies[-1].start()
         p_copies[-1].start()
-        s_copies[-1].start()
-
-    token = lax.broadcasted_iota(jnp.int32, (rows, NEW), 0) // QPK
-    fresh_at = lax.broadcasted_iota(jnp.int32, (rows, NEW), 1)
-    row_pos = jnp.zeros((rows, NEW), jnp.int32)
-    new_pos = jnp.zeros((rows, NEW), jnp.int32)
-    for t in range(NEW):
-        value = pos_ref[0, t]
-        row_pos = jnp.where(token == t, value, row_pos)
-        new_pos = jnp.where(fresh_at == t, value, new_pos)
-    allow = new_pos <= row_pos
-
-    q_copies[1].wait_recv()
-    local["k1"].wait()
-    local["fk"].wait()
-    query = qbuf[c]
-    top = scores(query, c)
-    fresh = lax.dot_general(
-        query, fkbuf[...], (((1,), (1,)), ((), ())), preferred_element_type=f32
-    )
-    fresh = jnp.where(allow, fresh, NEG)
-    top = jnp.maximum(top, jnp.max(fresh, axis=1, keepdims=True))
-    local["v1"].wait()
-    local["fv"].wait()
-    summed, total = weighted(rows, c, top)
-    fresh_weights = jnp.where(allow, jnp.exp2((fresh - top) * factor), 0.0).astype(bf16)
-    summed = summed + jnp.dot(fresh_weights, fvbuf[...], preferred_element_type=f32)
-    total = total + jnp.sum(fresh_weights.astype(f32), axis=1, keepdims=True)
-
-    for copy in p_copies + s_copies:
-        copy.wait_recv()
-    for side in range(2):
-        span = slice(side * half, (side + 1) * half)
-        top_here = jnp.broadcast_to(top[span], (half, 128))
+
+    token_here = lax.broadcasted_iota(jnp.int32, (half, NEW), 0) // QPK
+    fresh_at = lax.broadcasted_iota(jnp.int32, (half, NEW), 1)
+
+    def keep(at, side):
+        token = token_here + side * (half // QPK)
+        row_pos = jnp.zeros((half, NEW), jnp.int32)
+        new_pos = jnp.zeros((half, NEW), jnp.int32)
+        for t in range(NEW):
+            value = pos_ref[0, t]
+            row_pos = jnp.where(token == t, value, row_pos)
+            new_pos = jnp.where(fresh_at == t, value, new_pos)
+        allow = new_pos <= row_pos
+        query = qbuf[c, pl.ds(pl.multiple_of(side * half, half), half), :]
+        top = scores(query, c)
+        fresh = lax.dot_general(
+            query, fkbuf[...], (((1,), (1,)), ((), ())), preferred_element_type=f32
+        )
+        fresh = jnp.where(allow, fresh, NEG)
+        top = jnp.maximum(top, jnp.max(fresh, axis=1, keepdims=True))
+        if at == 0:
+            local["v1"].wait()
+            local["fv"].wait()
+        summed, total = weighted(half, c, top)
+        fresh_weights = jnp.where(allow, jnp.exp2((fresh - top) * factor), 0.0).astype(bf16)
+        summed = summed + jnp.dot(fresh_weights, fvbuf[...], preferred_element_type=f32)
+        total = total + jnp.sum(fresh_weights.astype(f32), axis=1, keepdims=True)
+        return jnp.broadcast_to(top, (half, 128)), total, summed
+
+    def merge(side, state):
+        top_here, total, summed = state
         top_there = jnp.transpose(jnp.broadcast_to(st_recv[side, 0:1, :], (128, half)))
         total_there = jnp.transpose(jnp.broadcast_to(st_recv[side, 8:9, :], (128, half)))
         best = jnp.maximum(top_here, top_there)
         here = jnp.exp2((top_here - best) * factor)
         there = jnp.exp2((top_there - best) * factor)
-        num = summed[span] * here + po_recv[side].astype(f32) * there
-        den = total[span] * here + total_there * there
-        fbuf[span, :] = num / den
+        num = summed * here + po_recv[side].astype(f32) * there
+        den = total * here + total_there * there
+        fbuf[pl.ds(pl.multiple_of(side * half, half), half), :] = num / den
+
+    local["q"].wait()
+    local["k0"].wait()
+    give_back(0, c)
+    local["k1"].wait()
+    local["fk"].wait()
+    state_mine = keep(0, c)
+    q_copies[0].wait_recv()
+    give_back(1, other)
+    q_copies[1].wait_recv()
+    state_other = keep(1, other)
+
+    s_copies[0].wait_recv()
+    p_copies[0].wait_recv()
+    merge(other, state_other)
+    s_copies[1].wait_recv()
+    p_copies[1].wait_recv()
+    merge(c, state_mine)
     for j in range(QPK):
         feature = fbuf[pl.ds(j, NEW, stride=QPK), :]
         gather[c, r, :, j * head_size : (j + 1) * head_size] = feature.astype(bf16)
@@ -285,7 +297,11 @@
     depth = out_weight.shape[0] // heads
     n_cols = width // COLS
     dma = pltpu.SemaphoreType.DMA
-    anywhere = pl.BlockSpec(memory_space=pl.ANY)
+    pinned = [
+        pltpu.with_memory_space_constraint(array, pltpu.HBM)
+        for array in (queries, cache_keys, cache_values, new_keys, new_values, positions)
+    ]
+    anywhere = pl.BlockSpec(memory_space=pltpu.HBM)
     scalars = pl.BlockSpec(memory_space=pltpu.SMEM)
     return pl.pallas_call(
         functools.partial(fused_kernel, n_head),
@@ -299,7 +315,7 @@
             pltpu.VMEM((NEW, head_size), bf16),
             pltpu.VMEM((NEW, head_size), bf16),
             pltpu.VMEM((heads, depth, width), bf16),
-            pltpu.VMEM((rows, slots), f32),
+            pltpu.VMEM((half, slots), f32),
             pltpu.VMEM((2, half, head_size), bf16),
             pltpu.VMEM((2, half, head_size), bf16),
             pltpu.VMEM((2, 16, half), f32),
@@ -322,7 +338,7 @@
             bytes_accessed=2 * heads * (2 * slots * head_size + depth * width),
             transcendentals=heads * rows * slots,
         ),
-    )(queries, cache_keys, cache_values, new_keys, new_values, lengths, positions, out_weight)
+    )(*pinned[:5], lengths, pinned[5], out_weight)
 
 
 def shifted(value, axis, steps):

time: 36.2 us -> 30.4 us (0.84)
  local copies, waits for them, and re-layouts: 6.33 us -> 0.63 us
    unnamed x13 -> x1, local copies, waits for them, and re-layouts: 6.33 us -> 0.63 us
where the time goes in v2:
time: 30.4 us; the launch traced here: 30.3 us
  Pallas kernels  29 us (95%)
  between operations  0.66 us (2%)
  local copies, waits for them, and re-layouts  0.63 us (2%)
    pallas_call x1, Pallas kernels, fused_body(): pl.pallas_call(functools.partial(fused_kernel, n_head), out_shape=jax.Sha...  29 us
    unnamed x1, local copies, waits for them, and re-layouts  0.63 us

profile of v2, /device:TPU:0, one launch (start us, length us, event | category | flops | bytes accessed | tf_op | source)
XLA Modules:
  0.0 30.3 jit_solution(15134846949159599618)
XLA Ops:
  0.7 29.0 %shard_map.82 = bf16[1,16,2048]{2,1,0:T(8,128)(2,1)S(1)} custom-call(bf16[1,2,128,128]{3,2,1,0:T(8,128)(2,1)} %q_hbm.1, bf16[1,2,3072,128]{3,2,1,0:T(8,128)(2,1)} %k_hbm.1, bf16[1,2,3072,128]{3,2,1,0:T(8,128)(2,1)} %v_hbm.1, bf16[1,2,16,128]{3,2,1,0:T(8,128)(2,1)} %fk_hbm.1, bf16[1,2,16,128]{3,2,1,0:T(8,128)(2,1)} %fv_hbm.1, s32[1]{0:T(128)S(6)} %copy.10.len_ref, ...), custom_call_target="tpu_custom_call" | custom-call | flops 1879048192 | bytes 19922944 | tf_op jit(solution)/shard_map/pallas_call | solution.py:306
  29.6 0.6 %copy.11 = bf16[1,16,2048]{2,1,0:T(8,128)(2,1)} copy(bf16[1,16,2048]{2,1,0:T(8,128)(2,1)S(1)} %shard_map.82) | data formatting | bytes 131072

commit v3 on v2

--- a/solution.py
+++ b/solution.py
@@ -22,11 +22,11 @@
 
 def fused_kernel(
     n_head,
-    q_hbm, k_hbm, v_hbm, fk_hbm, fv_hbm, len_ref, pos_ref, w_hbm,
+    q_hbm, k_hbm, v_hbm, fk_hbm, fv_hbm, len_ref, pos_hbm, w_hbm,
     out_ref,
-    qbuf, kbuf, vbuf, fkbuf, fvbuf, wbuf, sbuf,
+    pos_ref, qbuf, kbuf, vbuf, fkbuf, fvbuf, wbuf, sbuf,
     po_send, po_recv, st_send, st_recv, fbuf, gather, accbuf, rs_send, rs_recv,
-    q_sem, k_sem, v_sem, f_sem, w_sem,
+    q_sem, k_sem, v_sem, f_sem, n_sem, w_sem,
     qx_send, qx_recv, px_send, px_recv, sx_send, sx_recv,
     g_send, g_recv, rs_send_sem, rs_recv_sem,
 ):
@@ -58,6 +58,7 @@
     fetch("q", q_hbm.at[0], qbuf.at[:, mine, :], q_sem)
     fetch("k0", k_hbm.at[0, other], kbuf.at[other], k_sem.at[0])
     fetch("v0", v_hbm.at[0, other], vbuf.at[other], v_sem.at[0])
+    fetch("pos", pos_hbm, pos_ref, n_sem)
     fetch("k1", k_hbm.at[0, c], kbuf.at[c], k_sem.at[1])
     fetch("v1", v_hbm.at[0, c], vbuf.at[c], v_sem.at[1])
     fetch("fk", fk_hbm.at[0, c], fkbuf, f_sem.at[0])
@@ -90,6 +91,7 @@
                 w_sem.at[at, cut],
             )
 
+    local["pos"].wait()
     length = len_ref[0]
     first_slot = c * slots
 
@@ -223,6 +225,8 @@
     g_diag = pass_on(3, c, r, {"ctx": other, "roll": far})
     g_far.wait_recv()
     f_far = pass_on(4, c, far, {"roll": sib})
+    g_ctx.wait_recv()
+    f_ctx = pass_on(5, other, r, {"roll": sib})
     for at in range(2):
         for cut in range(WCUT):
             local[("w", at, cut)].wait()
@@ -238,13 +242,10 @@
             features, wbuf[head, :, at * COLS : (at + 1) * COLS], preferred_element_type=f32
         )
 
-    f_ctx = f_diag = None
+    f_diag = None
     for at in range(n_cols):
         accbuf[:, at * COLS : (at + 1) * COLS] = project(c, at)
         if at == n_cols // 2 - 1:
-            g_ctx.wait_recv()
-            f_ctx = pass_on(5, other, r, {"roll": sib})
-        if at == n_cols - 2:
             g_diag.wait_recv()
             f_diag = pass_on(6, other, far, {"roll": sib})
     f_ctx.wait_recv()
@@ -302,13 +303,13 @@
         for array in (queries, cache_keys, cache_values, new_keys, new_values, positions)
     ]
     anywhere = pl.BlockSpec(memory_space=pltpu.HBM)
-    scalars = pl.BlockSpec(memory_space=pltpu.SMEM)
     return pl.pallas_call(
         functools.partial(fused_kernel, n_head),
         out_shape=jax.ShapeDtypeStruct((1, NEW, width), bf16),
-        in_specs=[anywhere] * 5 + [scalars] * 2 + [anywhere],
+        in_specs=[anywhere] * 5 + [pl.BlockSpec(memory_space=pltpu.SMEM)] + [anywhere] * 2,
         out_specs=pl.BlockSpec(memory_space=pltpu.VMEM),
         scratch_shapes=[
+            pltpu.SMEM(positions.shape, positions.dtype),
             pltpu.VMEM((heads, rows, head_size), bf16),
             pltpu.VMEM((heads, slots, head_size), bf16),
             pltpu.VMEM((heads, slots, head_size), bf16),
@@ -325,7 +326,7 @@
             pltpu.VMEM((4 * NEW, width), f32),
             pltpu.VMEM((n_head, NEW, width), bf16),
             pltpu.VMEM((n_head - 1, NEW, width), bf16),
-            dma, dma((2,)), dma((2,)), dma((2,)), dma((2, WCUT)),
+            dma, dma((2,)), dma((2,)), dma((2,)), dma, dma((2, WCUT)),
             dma((2,)), dma((2,)), dma((2,)), dma((2,)), dma((2,)), dma((2,)),
             dma((7,)), dma((7,)),
             dma((n_head - 1, n_cols)), dma((n_head - 1, n_cols)),

time: 30.4 us -> 29.8 us (0.980)
  Pallas kernels: 29 us -> 28.4 us
    pallas_call x1, Pallas kernels: 29 us -> 28.4 us  [fused_body(): pl.pallas_call(functools.partial(fused_kernel, n_head), out_shape=jax.Sha...]
where the time goes in v3:
time: 29.8 us; the launch traced here: 29.7 us
  Pallas kernels  28.4 us (95%)
  between operations  0.66 us (2%)
  local copies, waits for them, and re-layouts  0.63 us (2%)
    pallas_call x1, Pallas kernels, fused_body(): pl.pallas_call(functools.partial(fused_kernel, n_head), out_shape=jax.Sha...  28.4 us
    unnamed x1, local copies, waits for them, and re-layouts  0.63 us

profile of v3, /device:TPU:0, one launch (start us, length us, event | category | flops | bytes accessed | tf_op | source)
XLA Modules:
  0.0 29.7 jit_solution(3302182779439186257)
XLA Ops:
  0.7 28.4 %shard_map.82 = bf16[1,16,2048]{2,1,0:T(8,128)(2,1)S(1)} custom-call(bf16[1,2,128,128]{3,2,1,0:T(8,128)(2,1)} %q_hbm.1, bf16[1,2,3072,128]{3,2,1,0:T(8,128)(2,1)} %k_hbm.1, bf16[1,2,3072,128]{3,2,1,0:T(8,128)(2,1)} %v_hbm.1, bf16[1,2,16,128]{3,2,1,0:T(8,128)(2,1)} %fk_hbm.1, bf16[1,2,16,128]{3,2,1,0:T(8,128)(2,1)} %fv_hbm.1, s32[1]{0:T(128)S(6)} %copy.10.len_ref, ...), custom_call_target="tpu_custom_call" | custom-call | flops 1879048192 | bytes 19922944 | tf_op jit(solution)/shard_map/pallas_call | solution.py:306
  29.1 0.6 %copy.11 = bf16[1,16,2048]{2,1,0:T(8,128)(2,1)} copy(bf16[1,16,2048]{2,1,0:T(8,128)(2,1)S(1)} %shard_map.82) | data formatting | bytes 131072

commit v4 on v3

--- a/solution.py
+++ b/solution.py
@@ -251,42 +251,71 @@
     f_ctx.wait_recv()
     f_diag.wait_recv()
 
+    odd = lax.rem(h, 2)
+    across, near = n_head - 1 - h, h + 1 - 2 * odd
+    middle = jnp.logical_and(h > 0, h < n_head - 1)
     rs_copies = []
+
+    def hand_over(at, block, to, slot):
+        span = slice(at * COLS, (at + 1) * COLS)
+        return pltpu.make_async_remote_copy(
+            src_ref=rs_send.at[block, :, span],
+            dst_ref=rs_recv.at[slot, :, span],
+            send_sem=rs_send_sem.at[slot, at],
+            recv_sem=rs_recv_sem.at[slot, at],
+            device_id={"head": to},
+            device_id_type=MESH,
+        )
+
+    def arrived(at, slot):
+        hand_over(at, across, across, slot).wait_recv()
+
+    def add_and_cross(at):
+        span = slice(at * COLS, (at + 1) * COLS)
+        arrived(at, 1)
+        theirs = pl.ds(pl.multiple_of(across * NEW, NEW), NEW)
+        part = accbuf[theirs, span] + rs_recv[1, :, span].astype(f32)
+        rs_send[across, :, span] = part.astype(bf16)
+        rs_copies[at][1].start()
+
     for at in range(n_cols):
         span = slice(at * COLS, (at + 1) * COLS)
         part = accbuf[:, span] + project(other, at)
         accbuf[:, span] = part
         rs_send[:, :, span] = part.astype(bf16).reshape(n_head, NEW, COLS)
-        for off in range(n_head - 1, 0, -1):
-            to = lax.rem(h + off, n_head)
-            copy = pltpu.make_async_remote_copy(
-                src_ref=rs_send.at[to, :, span],
-                dst_ref=rs_recv.at[off - 1, :, span],
-                send_sem=rs_send_sem.at[off - 1, at],
-                recv_sem=rs_recv_sem.at[off - 1, at],
-                device_id={"head": to},
-                device_id_type=MESH,
-            )
-            copy.start()
-            rs_copies.append((at, copy))
+        two = hand_over(at, lax.rem(h + 2, n_head), lax.rem(2 * h + 1, n_head + 1), 1)
+        cross = hand_over(at, across, across, 2 - 2 * odd)
+        side = hand_over(at, near, near, 2 * odd)
+        rs_copies.append((two, cross, side))
+        two.start()
+        pl.when(jnp.logical_not(middle))(cross.start)
+        side.start()
+        if at > 0:
+            pl.when(middle)(functools.partial(add_and_cross, at - 1))
+    pl.when(middle)(functools.partial(add_and_cross, n_cols - 1))
 
     own = pl.ds(pl.multiple_of(h * NEW, NEW), NEW)
+
+    def add_third(at):
+        span = slice(at * COLS, (at + 1) * COLS)
+        arrived(at, 1)
+        accbuf[own, span] += rs_recv[1, :, span].astype(f32)
+
     for at in range(n_cols):
         span = slice(at * COLS, (at + 1) * COLS)
-        for place, copy in rs_copies:
-            if place == at:
-                copy.wait_recv()
-        value = accbuf[own, span]
-        for off in range(n_head - 1):
-            value = value + rs_recv[off, :, span].astype(f32)
+        pl.when(jnp.logical_not(middle))(functools.partial(add_third, at))
+        arrived(at, 0)
+        arrived(at, 2)
+        value = accbuf[own, span] + rs_recv[0, :, span].astype(f32) + rs_recv[2, :, span].astype(f32)
         out_ref[0, :, span] = value.astype(bf16)
 
     for copy in q_copies + p_copies + s_copies:
         copy.wait_send()
     for copy in (g_far, g_sib, g_ctx, g_diag, f_far, f_ctx, f_diag):
         copy.wait_send()
-    for _, copy in rs_copies:
-        copy.wait_send()
+    for copies in rs_copies:
+        for copy in copies:
+            copy.wait_send()
 
 
 def fused_body(n_head, queries, cache_keys, cache_values, new_keys, new_values, lengths, positions, out_weight):

time: 29.8 us -> 30.6 us (1.027)
  Pallas kernels: 28.4 us -> 29.2 us
    pallas_call x1, Pallas kernels: 28.4 us -> 29.2 us  [fused_body(): pl.pallas_call(functools.partial(fused_kernel, n_head), out_shape=jax.Sha...]
where the time goes in v4:
time: 30.6 us; the launch traced here: 30.5 us
  Pallas kernels  29.2 us (95%)
  between operations  0.66 us (2%)
  local copies, waits for them, and re-layouts  0.63 us (2%)
    pallas_call x1, Pallas kernels, fused_body(): pl.pallas_call(functools.partial(fused_kernel, n_head), out_shape=jax.Sha...  29.2 us
    unnamed x1, local copies, waits for them, and re-layouts  0.63 us

profile of v4, /device:TPU:0, one launch (start us, length us, event | category | flops | bytes accessed | tf_op | source)
XLA Modules:
  0.0 30.5 jit_solution(8197637818574706399)
XLA Ops:
  0.7 29.2 %shard_map.82 = bf16[1,16,2048]{2,1,0:T(8,128)(2,1)S(1)} custom-call(bf16[1,2,128,128]{3,2,1,0:T(8,128)(2,1)} %q_hbm.1, bf16[1,2,3072,128]{3,2,1,0:T(8,128)(2,1)} %k_hbm.1, bf16[1,2,3072,128]{3,2,1,0:T(8,128)(2,1)} %v_hbm.1, bf16[1,2,16,128]{3,2,1,0:T(8,128)(2,1)} %fk_hbm.1, bf16[1,2,16,128]{3,2,1,0:T(8,128)(2,1)} %fv_hbm.1, s32[1]{0:T(128)S(6)} %copy.10.len_ref, ...), custom_call_target="tpu_custom_call" | custom-call | flops 1879048192 | bytes 19922944 | tf_op jit(solution)/shard_map/pallas_call | solution.py:335
  29.8 0.6 %copy.11 = bf16[1,16,2048]{2,1,0:T(8,128)(2,1)} copy(bf16[1,16,2048]{2,1,0:T(8,128)(2,1)S(1)} %shard_map.82) | data formatting | bytes 131072

commit v5 on v3

--- a/solution.py
+++ b/solution.py
@@ -17,7 +17,6 @@
 MESH = pl.DeviceIdType.MESH
 CHUNK = 512
 COLS = 512
-WCUT = 4
 
 
 def fused_kernel(
@@ -81,13 +80,13 @@
         q_copies[-1].start()
 
     depth = w_hbm.shape[0] // 2
-    piece = depth // WCUT
     for at, head in enumerate((c, other)):
-        for cut in range(WCUT):
+        for cut in range(wbuf.shape[2] // COLS):
+            span = pl.ds(cut * COLS, COLS)
             fetch(
                 ("w", at, cut),
-                w_hbm.at[pl.ds(pl.multiple_of(head * depth + cut * piece, piece), piece), :],
-                wbuf.at[head, pl.ds(cut * piece, piece), :],
+                w_hbm.at[pl.ds(pl.multiple_of(head * depth, depth), depth), span],
+                wbuf.at[head, :, span],
                 w_sem.at[at, cut],
             )
 
@@ -129,9 +128,6 @@
             local["v0"].wait()
         summed, total = weighted(half, other, top)
         po_send[side] = summed.astype(bf16)
-        turned = jnp.transpose(jnp.where(lane < 64, jnp.broadcast_to(top, (half, 128)), total))
-        st_send[side, 0:8, :] = turned[0:8, :]
-        st_send[side, 8:16, :] = turned[64:72, :]
         p_copies.append(
             pltpu.make_async_remote_copy(
                 src_ref=po_send.at[side], dst_ref=po_recv.at[side],
@@ -139,6 +135,10 @@
                 device_id=partner, device_id_type=MESH,
             )
         )
+        p_copies[-1].start()
+        turned = jnp.transpose(jnp.where(lane < 64, jnp.broadcast_to(top, (half, 128)), total))
+        st_send[side, 0:8, :] = turned[0:8, :]
+        st_send[side, 8:16, :] = turned[64:72, :]
         s_copies.append(
             pltpu.make_async_remote_copy(
                 src_ref=st_send.at[side], dst_ref=st_recv.at[side],
@@ -147,12 +147,11 @@
             )
         )
         s_copies[-1].start()
-        p_copies[-1].start()
 
     token_here = lax.broadcasted_iota(jnp.int32, (half, NEW), 0) // QPK
     fresh_at = lax.broadcasted_iota(jnp.int32, (half, NEW), 1)
 
-    def keep(at, side):
+    def new_mask(side):
         token = token_here + side * (half // QPK)
         row_pos = jnp.zeros((half, NEW), jnp.int32)
         new_pos = jnp.zeros((half, NEW), jnp.int32)
@@ -160,7 +159,9 @@
             value = pos_ref[0, t]
             row_pos = jnp.where(token == t, value, row_pos)
             new_pos = jnp.where(fresh_at == t, value, new_pos)
-        allow = new_pos <= row_pos
+        return new_pos <= row_pos
+
+    def keep(at, side, allow):
         query = qbuf[c, pl.ds(pl.multiple_of(side * half, half), half), :]
         top = scores(query, c)
         fresh = lax.dot_general(
@@ -193,11 +194,12 @@
     give_back(0, c)
     local["k1"].wait()
     local["fk"].wait()
-    state_mine = keep(0, c)
+    state_mine = keep(0, c, new_mask(c))
+    mask_other = new_mask(other)
     q_copies[0].wait_recv()
     give_back(1, other)
     q_copies[1].wait_recv()
-    state_other = keep(1, other)
+    state_other = keep(1, other, mask_other)
 
     s_copies[0].wait_recv()
     p_copies[0].wait_recv()
@@ -227,9 +229,6 @@
     f_far = pass_on(4, c, far, {"roll": sib})
     g_ctx.wait_recv()
     f_ctx = pass_on(5, other, r, {"roll": sib})
-    for at in range(2):
-        for cut in range(WCUT):
-            local[("w", at, cut)].wait()
     g_sib.wait_recv()
     f_far.wait_recv()
 
@@ -244,6 +243,7 @@
 
     f_diag = None
     for at in range(n_cols):
+        local[("w", 0, at)].wait()
         accbuf[:, at * COLS : (at + 1) * COLS] = project(c, at)
         if at == n_cols // 2 - 1:
             g_diag.wait_recv()
@@ -254,6 +254,7 @@
     rs_copies = []
     for at in range(n_cols):
         span = slice(at * COLS, (at + 1) * COLS)
+        local[("w", 1, at)].wait()
         part = accbuf[:, span] + project(other, at)
         accbuf[:, span] = part
         rs_send[:, :, span] = part.astype(bf16).reshape(n_head, NEW, COLS)
@@ -326,7 +327,7 @@
             pltpu.VMEM((4 * NEW, width), f32),
             pltpu.VMEM((n_head, NEW, width), bf16),
             pltpu.VMEM((n_head - 1, NEW, width), bf16),
-            dma, dma((2,)), dma((2,)), dma((2,)), dma, dma((2, WCUT)),
+            dma, dma((2,)), dma((2,)), dma((2,)), dma, dma((2, n_cols)),
             dma((2,)), dma((2,)), dma((2,)), dma((2,)), dma((2,)), dma((2,)),
             dma((7,)), dma((7,)),
             dma((n_head - 1, n_cols)), dma((n_head - 1, n_cols)),

time: 29.8 us -> 29.7 us (level)
  no operation moved by 1% of the time
where the time goes in v5:
time: 29.7 us; the launch traced here: 29.6 us
  Pallas kernels  28.3 us (95%)
  between operations  0.66 us (2%)
  local copies, waits for them, and re-layouts  0.63 us (2%)
    pallas_call x1, Pallas kernels, fused_body(): pl.pallas_call(functools.partial(fused_kernel, n_head), out_shape=jax.Sha...  28.3 us
    unnamed x1, local copies, waits for them, and re-layouts  0.63 us

profile of v5, /device:TPU:0, one launch (start us, length us, event | category | flops | bytes accessed | tf_op | source)
XLA Modules:
  0.0 29.6 jit_solution(9638469269280984318)
XLA Ops:
  0.7 28.3 %shard_map.82 = bf16[1,16,2048]{2,1,0:T(8,128)(2,1)S(1)} custom-call(bf16[1,2,128,128]{3,2,1,0:T(8,128)(2,1)} %q_hbm.1, bf16[1,2,3072,128]{3,2,1,0:T(8,128)(2,1)} %k_hbm.1, bf16[1,2,3072,128]{3,2,1,0:T(8,128)(2,1)} %v_hbm.1, bf16[1,2,16,128]{3,2,1,0:T(8,128)(2,1)} %fk_hbm.1, bf16[1,2,16,128]{3,2,1,0:T(8,128)(2,1)} %fv_hbm.1, s32[1]{0:T(128)S(6)} %copy.10.len_ref, ...), custom_call_target="tpu_custom_call" | custom-call | flops 1879048192 | bytes 19922944 | tf_op jit(solution)/shard_map/pallas_call | solution.py:307
  28.9 0.6 %copy.11 = bf16[1,16,2048]{2,1,0:T(8,128)(2,1)} copy(bf16[1,16,2048]{2,1,0:T(8,128)(2,1)S(1)} %shard_map.82) | data formatting | bytes 131072

commit v6 on v5

--- a/solution.py
+++ b/solution.py
@@ -16,7 +16,8 @@
 
 MESH = pl.DeviceIdType.MESH
 CHUNK = 512
-COLS = 512
+COLS = 256
+WIDE = 512
 
 
 def fused_kernel(
@@ -81,8 +82,8 @@
 
     depth = w_hbm.shape[0] // 2
     for at, head in enumerate((c, other)):
-        for cut in range(wbuf.shape[2] // COLS):
-            span = pl.ds(cut * COLS, COLS)
+        for cut in range(wbuf.shape[2] // WIDE):
+            span = pl.ds(cut * WIDE, WIDE)
             fetch(
                 ("w", at, cut),
                 w_hbm.at[pl.ds(pl.multiple_of(head * depth, depth), depth), span],
@@ -235,17 +236,18 @@
     n_cols = wbuf.shape[2] // COLS
     tokens = gather.shape[1] * NEW
 
-    def project(head, at):
+    def project(head, at, step):
         features = gather[head].reshape(tokens, depth)
         return jnp.dot(
-            features, wbuf[head, :, at * COLS : (at + 1) * COLS], preferred_element_type=f32
+            features, wbuf[head, :, at * step : (at + 1) * step], preferred_element_type=f32
         )
 
     f_diag = None
-    for at in range(n_cols):
+    n_wide = wbuf.shape[2] // WIDE
+    for at in range(n_wide):
         local[("w", 0, at)].wait()
-        accbuf[:, at * COLS : (at + 1) * COLS] = project(c, at)
-        if at == n_cols // 2 - 1:
+        accbuf[:, at * WIDE : (at + 1) * WIDE] = project(c, at, WIDE)
+        if at == n_wide // 2 - 1:
             g_diag.wait_recv()
             f_diag = pass_on(6, other, far, {"roll": sib})
     f_ctx.wait_recv()
@@ -254,8 +256,9 @@
     rs_copies = []
     for at in range(n_cols):
         span = slice(at * COLS, (at + 1) * COLS)
-        local[("w", 1, at)].wait()
-        part = accbuf[:, span] + project(other, at)
+        if at * COLS % WIDE == 0:
+            local[("w", 1, at * COLS // WIDE)].wait()
+        part = accbuf[:, span] + project(other, at, COLS)
         accbuf[:, span] = part
         rs_send[:, :, span] = part.astype(bf16).reshape(n_head, NEW, COLS)
         for off in range(n_head - 1, 0, -1):
@@ -327,7 +330,7 @@
             pltpu.VMEM((4 * NEW, width), f32),
             pltpu.VMEM((n_head, NEW, width), bf16),
             pltpu.VMEM((n_head - 1, NEW, width), bf16),
-            dma, dma((2,)), dma((2,)), dma((2,)), dma, dma((2, n_cols)),
+            dma, dma((2,)), dma((2,)), dma((2,)), dma, dma((2, width // WIDE)),
             dma((2,)), dma((2,)), dma((2,)), dma((2,)), dma((2,)), dma((2,)),
             dma((7,)), dma((7,)),
             dma((n_head - 1, n_cols)), dma((n_head - 1, n_cols)),

time: 29.7 us -> 29.9 us (level)
  no operation moved by 1% of the time
where the time goes in v6:
time: 29.9 us; the launch traced here: 29.8 us
  Pallas kernels  28.5 us (95%)
  between operations  0.66 us (2%)
  local copies, waits for them, and re-layouts  0.63 us (2%)
    pallas_call x1, Pallas kernels, fused_body(): pl.pallas_call(functools.partial(fused_kernel, n_head), out_shape=jax.Sha...  28.5 us
    unnamed x1, local copies, waits for them, and re-layouts  0.63 us

profile of v6, /device:TPU:0, one launch (start us, length us, event | category | flops | bytes accessed | tf_op | source)
XLA Modules:
  0.0 29.8 jit_solution(2776366230508157972)
XLA Ops:
  0.7 28.5 %shard_map.82 = bf16[1,16,2048]{2,1,0:T(8,128)(2,1)S(1)} custom-call(bf16[1,2,128,128]{3,2,1,0:T(8,128)(2,1)} %q_hbm.1, bf16[1,2,3072,128]{3,2,1,0:T(8,128)(2,1)} %k_hbm.1, bf16[1,2,3072,128]{3,2,1,0:T(8,128)(2,1)} %v_hbm.1, bf16[1,2,16,128]{3,2,1,0:T(8,128)(2,1)} %fk_hbm.1, bf16[1,2,16,128]{3,2,1,0:T(8,128)(2,1)} %fv_hbm.1, s32[1]{0:T(128)S(6)} %copy.10.len_ref, ...), custom_call_target="tpu_custom_call" | custom-call | flops 1879048192 | bytes 19922944 | tf_op jit(solution)/shard_map/pallas_call | solution.py:310
  29.1 0.6 %copy.11 = bf16[1,16,2048]{2,1,0:T(8,128)(2,1)} copy(bf16[1,16,2048]{2,1,0:T(8,128)(2,1)S(1)} %shard_map.82) | data formatting | bytes 131072
